TPU v7x, 32 devices: a whole 2x2x4 slice. The times are simulated.
32 devices in a mesh: seq: 16 (over z, x, core), head: 2 (over y).
Axes of the slice: x: 2, y: 2, z: 4, core: 2. Of those that a mesh axis runs over, the one named last changes fastest.
Arguments:
- queries: bfloat16 [32768, 2048], P(('seq', 'head'))
- span_keys: bfloat16 [32768, 1024], P(('seq', 'head'))
- span_values: bfloat16 [32768, 1024], P(('seq', 'head')), may hold values from -6 to 6
- head_gates: bfloat16 [32768, 16], P(('seq', 'head')), may hold values from -8 to 8
- query_gain: float32 [128], replicated, may hold values from 0.5 to 5
- key_gain: float32 [128], replicated, may hold values from 0.5 to 5
- prompt_keys: bfloat16 [2, 1024, 8, 128], P(None, 'seq', 'head'), may hold values from -6 to 6
- prompt_values: bfloat16 [2, 1024, 8, 128], P(None, 'seq', 'head'), may hold values from -6 to 6
- prompt_length: int32 [2], replicated, may hold values from 1 to 1024, as said below
- request_group: int32 [16], replicated, may hold values from 0 to 1, as said below
Outputs:
- attended: bfloat16 [32768, 2048], P(('seq', 'head'))
- cache_keys: bfloat16 [16, 3072, 8, 128], P('seq', None, 'head')
- cache_values: bfloat16 [16, 3072, 8, 128], P('seq', None, 'head')
Inputs may be any that keep to these rules, and one draw needn't show every extreme that they name: `prompt_length`: the largest length equals 1024 for some prompt. `request_group`: every prompt is used by at least one request.
All inputs are finite; a program needn't handle non-finite values.
Results may differ from a plain program's by a relative error of at most 0.0033.
The roundings to bfloat16 on the way count: a program that leaves them out, or rounds other values in their place, can miss the bound.
Values may be sent and summed in bfloat16 or wider, within the bound.
A program may use at most 128 MiB of HBM per device.

v0:
```python
import math

import jax
import jax.numpy as jnp
from jax import lax
from jax.sharding import PartitionSpec as P

QH = 16
KVH = 8
HD = 128


def norm_rope(values_in, gain_vec, positions):
    head_dim = values_in.shape[-1]
    half_dim = head_dim // 2
    upcast = values_in.astype(jnp.float32)
    mean_sq = jnp.mean(upcast * upcast, axis=-1, keepdims=True) + 1e-06
    normed = upcast * lax.rsqrt(mean_sq) * gain_vec
    inv_freq = jnp.exp(
        -(jnp.arange(half_dim, dtype=jnp.float32) * (2.0 / head_dim)) * math.log(1000000.0)
    )
    angles = positions[:, None] * inv_freq[None, :]
    cosine = jnp.cos(angles)[:, None, :]
    sine_part = jnp.sin(angles)[:, None, :]
    first_half = normed[..., :half_dim]
    second_half = normed[..., half_dim:]
    rotated = jnp.concatenate(
        [
            first_half * cosine - second_half * sine_part,
            second_half * cosine + first_half * sine_part,
        ],
        axis=-1,
    )
    return rotated.astype(jnp.bfloat16)


def attend(rotated_q, keys_all, values_all, gate_logits, length, cache_len):
    rows_total, kv_count, per_kv, head_dim = rotated_q.shape
    key_count = keys_all.shape[0]
    block_rows = min(512, rows_total)
    blocks = rows_total // block_rows
    key_pos = jnp.arange(key_count, dtype=jnp.int32)
    scale = 1.0 / math.sqrt(head_dim)

    def one_block(position):
        head_index = position // blocks
        row_start = position % blocks * block_rows
        kv_index = head_index // per_kv
        sub_index = head_index % per_kv
        query_block = lax.dynamic_slice(
            rotated_q, (row_start, kv_index, sub_index, jnp.int32(0)), (block_rows, 1, 1, head_dim)
        ).reshape(block_rows, head_dim)
        key_head = lax.dynamic_index_in_dim(keys_all, kv_index, 1, keepdims=False)
        value_head = lax.dynamic_index_in_dim(values_all, kv_index, 1, keepdims=False)
        gate_block = lax.dynamic_slice(
            gate_logits, (row_start, kv_index, sub_index), (block_rows, 1, 1)
        ).reshape(block_rows, 1)
        scores = (
            lax.dot_general(
                query_block, key_head, (((1,), (1,)), ((), ())), preferred_element_type=jnp.float32
            )
            * scale
        )
        row_ids = row_start + jnp.arange(block_rows, dtype=jnp.int32)
        allowed = jnp.where(
            key_pos[None, :] < cache_len,
            key_pos[None, :] < length,
            key_pos[None, :] - cache_len <= row_ids[:, None],
        )
        scores = jnp.where(allowed, scores, -1e30)
        top_score = jnp.max(scores, axis=-1, keepdims=True)
        raised = jnp.exp(scores - top_score)
        weights = (raised / jnp.sum(raised, axis=-1, keepdims=True)).astype(jnp.bfloat16)
        mixed_out = jnp.dot(weights, value_head, preferred_element_type=jnp.float32)
        return (mixed_out * jax.nn.sigmoid(gate_block.astype(jnp.float32))).astype(jnp.bfloat16)

    outputs = lax.map(one_block, jnp.arange(kv_count * per_kv * blocks, dtype=jnp.int32))
    outputs = outputs.reshape(kv_count, per_kv, blocks, block_rows, head_dim)
    return outputs.transpose(2, 3, 0, 1, 4).reshape(rows_total, kv_count, per_kv, head_dim)


def append_span(prefix, span_rows, length):
    cache_len = prefix.shape[0]
    slot_pos = jnp.arange(cache_len, dtype=jnp.int32)
    kept = jnp.where((slot_pos < length)[:, None, None], prefix, jnp.zeros_like(prefix))
    base = jnp.concatenate([kept, jnp.zeros_like(span_rows)], axis=0)
    return lax.dynamic_update_slice_in_dim(base, span_rows, length, 0)


def on_device(
    queries,
    span_keys,
    span_values,
    head_gates,
    query_gain,
    key_gain,
    prompt_keys,
    prompt_values,
    prompt_length,
    request_group,
):
    per_kv = QH // KVH
    local_rows = queries.shape[0]
    query_split = queries.reshape(local_rows, KVH, per_kv * HD)
    key_split = span_keys.reshape(local_rows, KVH, HD)
    value_split = span_values.reshape(local_rows, KVH, HD)
    gate_split = head_gates.reshape(local_rows, KVH, per_kv)
    query_rows, key_rows, value_rows, gate_rows = (
        lax.all_to_all(query_split, "head", split_axis=1, concat_axis=0, tiled=True),
        lax.all_to_all(key_split, "head", split_axis=1, concat_axis=0, tiled=True),
        lax.all_to_all(value_split, "head", split_axis=1, concat_axis=0, tiled=True),
        lax.all_to_all(gate_split, "head", split_axis=1, concat_axis=0, tiled=True),
    )
    span_len = query_rows.shape[0]
    kv_local = key_rows.shape[1]
    seq_index = lax.axis_index("seq")
    group = lax.dynamic_index_in_dim(request_group, seq_index, 0, keepdims=False)
    length = lax.dynamic_index_in_dim(prompt_length, group, 0, keepdims=False)
    every_k, every_v = (
        lax.all_gather(prompt_keys, "seq", axis=1, tiled=True),
        lax.all_gather(prompt_values, "seq", axis=1, tiled=True),
    )
    prefix_k = lax.dynamic_index_in_dim(every_k, group, 0, keepdims=False)
    prefix_v = lax.dynamic_index_in_dim(every_v, group, 0, keepdims=False)
    cache_len = prefix_k.shape[0]
    positions = (length + jnp.arange(span_len, dtype=jnp.int32)).astype(jnp.float32)
    rotated_q = norm_rope(
        query_rows.reshape(span_len, kv_local * per_kv, HD), query_gain, positions
    ).reshape(span_len, kv_local, per_kv, HD)
    rotated_k = norm_rope(key_rows, key_gain, positions)
    keys_all = jnp.concatenate([prefix_k, rotated_k], axis=0)
    values_all = jnp.concatenate([prefix_v, value_rows], axis=0)
    result = attend(rotated_q, keys_all, values_all, gate_rows, length, cache_len)
    result = result.reshape(span_len, kv_local, per_kv * HD)
    back_rows = lax.all_to_all(result, "head", split_axis=0, concat_axis=1, tiled=True)
    attended = back_rows.reshape(local_rows, QH * HD)
    new_keys = append_span(prefix_k, rotated_k, length)[None]
    new_values = append_span(prefix_v, value_rows, length)[None]
    return (attended, new_keys, new_values)


def solution(mesh):
    placed = (
        P(("seq", "head"), None),
        P(("seq", "head"), None),
        P(("seq", "head"), None),
        P(("seq", "head"), None),
        P(),
        P(),
        P(None, "seq", "head", None),
        P(None, "seq", "head", None),
        P(),
        P(),
    )
    return jax.shard_map(
        on_device,
        mesh=mesh,
        in_specs=placed,
        out_specs=(
            P(("seq", "head"), None),
            P("seq", None, "head", None),
            P("seq", None, "head", None),
        ),
        check_vma=False,
    )
```

profile of v0, /device:TPU:0, one launch (start us, length us, event | category | flops | bytes accessed | tf_op | source)
XLA Modules:
  0.0 653.9 jit_solution(10141495754640683229)
XLA Ops:
  9.3 4.2 all-to-all-start.3
  13.5 3.9 copy.125
  21.3 3.9 copy.129
  25.2 21.4 %all-to-all-done.1 = bf16[1024,8,128]{0,2,1:T(8,128)(2,1)S(1)} async-done(((bf16[1024,8,128]{0,2,1:T(8,128)(2,1)}), bf16[1024,8,128]{0,2,1:T(8,128)(2,1)S(1)}, u32[]{:S(2)}, u32[]{:S(2)}) %all-to-all-start.1) | async-done | bytes 2097184 | tf_op jit(solution)/shard_map/all_to_all | solution.py:110
  46.6 4.8 all-to-all-start.2
  54.1 6.4 copy.117
  62.3 13.8 %all-to-all-done.2 = bf16[1024,8,128]{0,2,1:T(8,128)(2,1)} async-done(((bf16[1024,8,128]{0,2,1:T(8,128)(2,1)}), bf16[1024,8,128]{0,2,1:T(8,128)(2,1)}, u32[]{:S(2)}, u32[]{:S(2)}) %all-to-all-start.2) | async-done | bytes 2097184 | tf_op jit(solution)/shard_map/all_to_all | solution.py:111
  76.2 5.7 all-to-all-start
  81.8 5.3 multiply_cosine_fusion
  90.2 5.4 copy.127
  95.6 4.2 fusion.16
  102.8 5.7 subtract_convert_fusion.1
  108.5 19.5 %all-to-all-done = bf16[1024,8,256]{0,2,1:T(8,128)(2,1)} async-done(((bf16[1024,8,256]{0,2,1:T(8,128)(2,1)}), bf16[1024,8,256]{0,2,1:T(8,128)(2,1)}, u32[]{:S(2)}, u32[]{:S(2)}) %all-to-all-start) | async-done | bytes 4194336 | tf_op jit(solution)/shard_map/all_to_all | solution.py:109
  128.1 6.5 convert_element_type.90
  134.6 9.9 %copy.119 = f32[2,1024,4,256]{3,2,1,0:T(4,128)} copy(f32[2,1024,4,256]{1,3,2,0:T(8,128)} %bitcast.93) | data formatting | bytes 16777216 | tf_op jit(solution)/shard_map/convert_element_type | solution.py:16
  144.5 10.3 %reshape.231 = f32[2048,8,128]{2,1,0:T(8,128)} reshape(f32[2,1024,4,256]{3,2,1,0:T(4,128)} %copy.119) | data formatting | bytes 16777216 | tf_op jit(solution)/shard_map/convert_element_type | solution.py:16
  154.8 6.6 %multiply_reduce_fusion = f32[2048,8]{1,0:T(8,128)} fusion(f32[2048,8,128]{2,1,0:T(8,128)} %reshape.231), kind=kLoop, calls=%fused_computation.26 | loop fusion | flops 4177920 | bytes 8454144 | tf_op jit(solution)/shard_map/reduce_sum | solution.py:17
  164.3 6.9 %multiply_multiply_fusion = f32[2048,8,128]{2,1,0:T(8,128)S(1)} fusion(f32[2048,8,128]{2,1,0:T(8,128)} %reshape.231, f32[128]{0:T(128)S(1)} %copy-done.5, f32[2048,8]{1,0:T(8,128)} %copy.121), kind=kLoop, calls=%fused_computation.25 | loop fusion | flops 4194304 | bytes 16843264 | tf_op jit(solution)/shard_map/mul | solution.py:18
  171.1 5.5 subtract_convert_fusion
  195.2 357.0 %while.15 = (s32[]{:T(128)}, bf16[32,512,128]{2,1,0:T(8,128)(2,1)}, s32[]{:T(128)}, s32[32]{0:T(128)S(1)}, bf16[2048,4,2,128]{3,0,2,1:T(8,128)(2,1)}, /*index=5*...) while((s32[]{:T(128)}, bf16[32,512,128]{2,1,0:T(8,128)(2,1)}, ...), condition=%wide.region_5.6_spmd.clone.clone, body=%wide.region_2.5_spmd.clone.clone.sunk | while | flops 821176896 | bytes 20768428 | solution.py:77
  552.2 8.5 %copy.153 = bf16[4,2,4,512,128]{4,1,3,2,0:T(2,128)(2,1)} copy(bf16[4,2,4,512,128]{4,3,2,1,0:T(8,128)(2,1)} %bitcast.107) | data formatting | bytes 8388608 | tf_op jit(solution)/shard_map/reshape | solution.py:78
  560.6 7.6 %reshape_reshape.3 = bf16[2048,4,256]{2,0,1:T(8,128)(2,1)} reshape(bf16[4,512,4,2,128]{4,3,1,0,2:T(2,128)(2,1)} %bitcast.100) | data formatting | bytes 8388608 | tf_op jit(solution)/shard_map/reshape;reshape | solution.py:134
  568.2 7.6 %copy.134 = bf16[2048,4,256]{2,1,0:T(4,128)(2,1)} copy(bf16[2048,4,256]{2,0,1:T(8,128)(2,1)} %reshape_reshape.3) | data formatting | bytes 8388608 | tf_op jit(solution)/shard_map/reshape;reshape | solution.py:134
  575.8 5.6 all-to-all-start.4
  583.8 4.7 pad_maximum_fusion.2
  592.4 12.6 %dynamic_update_slice.16 = bf16[1,3072,4,128]{3,1,2,0:T(8,128)(2,1)} dynamic-update-slice(bf16[1,3072,4,128]{3,1,2,0:T(8,128)(2,1)} %get-tuple-element.264, bf16[1,2048,4,128]{3,1,2,0:T(8,128)(2,1)} %pad_maximum_fusion.2, s32[]{:T(128)} %constant.178.clone.1, s32[]{:T(128)S(6)} %select_n.106, s32[]{:T(128)} %constant.178.clone.1, s32[]{:T(128)} %constant.178.clone.1) | dynamic-update-slice | bytes 4194308 | tf_op jit(solution)/shard_map/dynamic_update_slice | solution.py:87
  605.0 6.2 copy.139
  611.3 12.1 %dynamic_update_slice.17 = bf16[1,3072,4,128]{3,1,2,0:T(8,128)(2,1)} dynamic-update-slice(bf16[1,3072,4,128]{3,1,2,0:T(8,128)(2,1)} %get-tuple-element.263, bf16[1,2048,4,128]{3,1,2,0:T(8,128)(2,1)S(1)} %bitcast.95, s32[]{:T(128)} %constant.178.clone.1, s32[]{:T(128)S(6)} %select_n.106, s32[]{:T(128)} %constant.178.clone.1, s32[]{:T(128)} %constant.178.clone.1) | dynamic-update-slice | bytes 4194308 | tf_op jit(solution)/shard_map/dynamic_update_slice | solution.py:87
  623.3 6.2 copy.140
  629.6 4.7 copy.135
  634.3 6.3 copy.136
  640.6 6.4 copy.138
  (311 shorter events, 308.0 us)
Async XLA Ops:
  7.2 176.5 %all-gather.5.cloned.1.call-start = ((), (), s32[]{:S(2)}) async-start(), calls=%async_computation.6 | async-start | bytes 2228224 | tf_op jit(solution)/shard_map/all_gather | solution.py:121
  9.3 8.2 %all-to-all-start.3 = ((bf16[1024,8,2]{0,2,1:T(2,128)(2,1)}), bf16[1024,8,2]{0,2,1:T(2,128)(2,1)S(1)}, u32[]{:S(2)}, u32[]{:S(2)}) async-start(bf16[1024,8,2]{0,2,1:T(2,128)(2,1)} %reshape.225), calls=%async_computation.3 | async-start | bytes 65536 | tf_op jit(solution)/shard_map/all_to_all | solution.py:112
  17.5 29.1 %all-to-all-start.1 = ((bf16[1024,8,128]{0,2,1:T(8,128)(2,1)}), bf16[1024,8,128]{0,2,1:T(8,128)(2,1)S(1)}, u32[]{:S(2)}, u32[]{:S(2)}) async-start(bf16[1024,8,128]{0,2,1:T(8,128)(2,1)} %bitcast.106), calls=%async_computation.1 | async-start | bytes 4194304 | tf_op jit(solution)/shard_map/all_to_all | solution.py:110
  21.3 30.9 %copy-start.7 = (s32[16]{0:T(128)S(1)}, s32[16]{0:T(128)}, u32[]{:S(2)}) copy-start(s32[16]{0:T(128)} %param.21) | copy-start | bytes 196
  46.6 29.5 %all-to-all-start.2 = ((bf16[1024,8,128]{0,2,1:T(8,128)(2,1)}), bf16[1024,8,128]{0,2,1:T(8,128)(2,1)}, u32[]{:S(2)}, u32[]{:S(2)}) async-start(bf16[1024,8,128]{0,2,1:T(8,128)(2,1)} %bitcast.105), calls=%async_computation.2 | async-start | bytes 4194304 | tf_op jit(solution)/shard_map/all_to_all | solution.py:111
  51.4 134.9 %all-gather.3.cloned.1.call-start = ((), (), s32[]{:S(2)}) async-start(), calls=%async_computation.5 | async-start | bytes 2228224 | tf_op jit(solution)/shard_map/all_gather | solution.py:120
  54.1 7.1 %copy-start.8 = (s32[2]{0:T(128)S(1)}, s32[2]{0:T(128)}, u32[]{:S(2)}) copy-start(s32[2]{0:T(128)} %param.20) | copy-start | bytes 28
  76.2 51.9 %all-to-all-start = ((bf16[1024,8,256]{0,2,1:T(8,128)(2,1)}), bf16[1024,8,256]{0,2,1:T(8,128)(2,1)}, u32[]{:S(2)}, u32[]{:S(2)}) async-start(bf16[1024,8,256]{0,2,1:T(8,128)(2,1)} %bitcast.98), calls=%async_computation | async-start | bytes 8388608 | tf_op jit(solution)/shard_map/all_to_all | solution.py:109
  90.2 5.4 copy-start.6
  154.8 9.5 %copy-start.5 = (f32[128]{0:T(128)S(1)}, f32[128]{0:T(128)}, u32[]{:S(2)}) copy-start(f32[128]{0:T(128)} %param.16) | copy-start | bytes 1540
  186.3 2.9 copy-start.4
  188.0 1.1 copy-start.2
  189.1 2.2 copy-start
  189.1 3.4 copy-start.1
  575.8 53.7 %all-to-all-start.4 = ((bf16[2048,4,256]{2,1,0:T(4,128)(2,1)}), bf16[2048,4,256]{2,1,0:T(4,128)(2,1)}, u32[]{:S(2)}, u32[]{:S(2)}) async-start(bf16[2048,4,256]{2,1,0:T(4,128)(2,1)} %copy.134), calls=%async_computation.4 | async-start | bytes 8388608 | tf_op jit(solution)/shard_map/all_to_all | solution.py:135
  583.1 5.4 copy-start.3
Sparse Core Ops, SparseCore 0:
  10.2 44.0 all-gather.4
  56.5 41.1 all-gather.2
where the time goes:
time: 661 us; the launch traced here: 654 us
  matrix products  193 us (29%)
  local copies, waits for them, and re-layouts  161 us (24%)
  other arithmetic  112 us (17%)
  loops' own time  89.2 us (13%)
  waiting for transfers between devices  56.1 us (8%)
  starting transfers between devices  24.2 us (4%)
  between operations  17.9 us (3%)
    dot_general x32, matrix products, one_block(): lax.dot_general(query_block, key_head, (((1,), (1,)), ((), ())), preferre...  97.2 us
    dot_general x32, matrix products, one_block(): mixed_out = jnp.dot(weights, value_head, preferred_element_type=jnp.float32)  96.3 us
    another operation x1, loops' own time, attend(): lax.map(one_block, jnp.arange(kv_count * per_kv * blocks, dtype=jnp.int32))  89.2 us
    unnamed x24, local copies, waits for them, and re-layouts  35.6 us
    reduce_sum x32, other arithmetic, one_block(): jnp.sum(raised, axis=-1, keepdims=True)  31.9 us
    convert_element_type x3, local copies, waits for them, and re-layouts, norm_rope(): upcast = values_in.astype(jnp.float32)  25.6 us
    dynamic_update_slice x2, local copies, waits for them, and re-layouts, append_span(): return lax.dynamic_update_slice_in_dim(base, span_rows, length, 0)  24.7 us
    all_to_all x1, waiting for transfers between devices, on_device(): lax.all_to_all(key_split, 'head', split_axis=1, concat_axis=0, tiled=True)  21.4 us
  transfers between devices with their start and end apart: 7, of which 3 were waited for; matrix products, arithmetic and copies ran while one was open for 23% of the time, Pallas kernels for 0%

commit v1 on v0

v1 whole, which is shorter than its diff:
```python
import functools
import math

import jax
import jax.numpy as jnp
from jax import lax
from jax.experimental import pallas as pl
from jax.experimental.pallas import tpu as pltpu
from jax.sharding import PartitionSpec as P

QH = 16
KVH = 8
HD = 128
PER = QH // KVH
BQ = 256
LOG2E = 1.4426950408889634


def norm_rope(x, gain, cosine, sine):
    x = x.astype(jnp.float32)
    mean_sq = jnp.mean(x * x, axis=-1, keepdims=True) + 1e-06
    n = x * lax.rsqrt(mean_sq) * gain
    return (n * cosine + pltpu.roll(n, HD // 2, 1) * sine).astype(jnp.bfloat16)


def attend_kernel(
    first_head,
    length_ref,
    rows_ref,
    prompt_ref,
    gate_ref,
    qgain_ref,
    kgain_ref,
    cos_ref,
    sin_ref,
    out_ref,
    key_ref,
):
    span = rows_ref.shape[0]
    cache_len = prompt_ref.shape[1]
    length = length_ref[0]
    head0 = length_ref[1] + first_head
    bq = min(BQ, span)
    blocks = span // bq
    const = LOG2E / math.sqrt(HD)

    @pl.loop(0, blocks)
    def _(i):
        at = pl.ds(pl.multiple_of(i * bq, bq), bq)
        key_ref[at, :] = norm_rope(
            rows_ref[at, PER * HD : (PER + 1) * HD], kgain_ref[...], cos_ref[at, :], sin_ref[at, :]
        )

    bias = jnp.where(lax.broadcasted_iota(jnp.int32, (1, cache_len), 1) < length, 0.0, -1e30)
    tri = lax.broadcasted_iota(jnp.int32, (bq, bq), 1) <= lax.broadcasted_iota(
        jnp.int32, (bq, bq), 0
    )
    nt = (((1,), (1,)), ((), ()))

    def scores(i, sub):
        at = slice(i * bq, (i + 1) * bq)
        q = norm_rope(
            rows_ref[at, sub * HD : (sub + 1) * HD], qgain_ref[...], cos_ref[at, :], sin_ref[at, :]
        )
        parts = [
            lax.dot_general(q, prompt_ref[0], nt, preferred_element_type=jnp.float32) + bias
        ]
        if i > 0:
            parts.append(
                lax.dot_general(q, key_ref[: i * bq, :], nt, preferred_element_type=jnp.float32)
            )
        diag = lax.dot_general(q, key_ref[at, :], nt, preferred_element_type=jnp.float32)
        parts.append(jnp.where(tri, diag, -1e30))
        top = functools.reduce(
            jnp.maximum, [jnp.max(p, axis=-1, keepdims=True) for p in parts]
        )
        return parts, top

    def finish(i, sub, parts, top):
        at = slice(i * bq, (i + 1) * bq)
        raised = [jnp.exp2((p - top) * const) for p in parts]
        total = sum(jnp.sum(p, axis=-1, keepdims=True) for p in raised)
        inverse = 1.0 / total
        weights = [(p * inverse).astype(jnp.bfloat16) for p in raised]
        vcol = slice((PER + 1) * HD, (PER + 2) * HD)
        values = [prompt_ref[1]]
        if i > 0:
            values.append(rows_ref[: i * bq, vcol])
        values.append(rows_ref[at, vcol])
        mixed = sum(
            jnp.dot(w, v, preferred_element_type=jnp.float32) for w, v in zip(weights, values)
        )
        gates = gate_ref[at, :].astype(jnp.float32)
        lane = lax.broadcasted_iota(jnp.int32, gates.shape, 1)
        gate = jnp.sum(jnp.where(lane == head0 + sub, gates, 0.0), axis=-1, keepdims=True)
        out_ref[at, sub * HD : (sub + 1) * HD] = (mixed * jax.nn.sigmoid(gate)).astype(
            jnp.bfloat16
        )

    for i in range(blocks):
        work = [(i, sub) + scores(i, sub) for sub in range(PER)]
        for item in work:
            finish(*item)


def attend(first_head, scalars, rows, prompt, gates, qgain, kgain, cosine, sine):
    span = rows.shape[0]
    cache_len = prompt.shape[1]
    vmem = pl.BlockSpec(memory_space=pltpu.VMEM)
    pairs = PER * span * (cache_len + span // 2)
    return pl.pallas_call(
        functools.partial(attend_kernel, first_head),
        out_shape=(
            jax.ShapeDtypeStruct((span, PER * HD), jnp.bfloat16),
            jax.ShapeDtypeStruct((span, HD), jnp.bfloat16),
        ),
        in_specs=[pl.BlockSpec(memory_space=pltpu.SMEM)] + [vmem] * 7,
        out_specs=(vmem, vmem),
        compiler_params=pltpu.CompilerParams(vmem_limit_bytes=48 * 1024 * 1024),
        cost_estimate=pl.CostEstimate(
            flops=8 * pairs * HD, bytes_accessed=6 * span * HD * 4, transcendentals=pairs
        ),
    )(scalars, rows, prompt, gates, qgain, kgain, cosine, sine)


def append_span(prefix, span_rows, length):
    cache_len = prefix.shape[0]
    slot_pos = jnp.arange(cache_len, dtype=jnp.int32)
    kept = jnp.where((slot_pos < length)[:, None], prefix, jnp.zeros_like(prefix))
    base = jnp.concatenate([kept, jnp.zeros_like(span_rows)], axis=0)
    return lax.dynamic_update_slice_in_dim(base, span_rows, length, 0)


def on_device(
    queries,
    span_keys,
    span_values,
    head_gates,
    query_gain,
    key_gain,
    prompt_keys,
    prompt_values,
    prompt_length,
    request_group,
):
    n = lax.axis_size("head")
    rows = queries.shape[0]
    span = rows * n
    kvl = KVH // n
    groups, part, _, _ = prompt_keys.shape
    group = lax.dynamic_index_in_dim(request_group, lax.axis_index("seq"), 0, keepdims=False)
    length = lax.dynamic_index_in_dim(prompt_length, group, 0, keepdims=False)
    scalars = jnp.stack([length, lax.axis_index("head") * (kvl * PER)]).astype(jnp.int32)

    gates = lax.all_gather(head_gates, "head", axis=0, tiled=True)
    received, prompts = [], []
    for c in range(kvl):
        pieces = []
        for d in range(n):
            head = d * kvl + c
            pieces.append(
                jnp.concatenate(
                    [
                        queries[:, head * PER * HD : (head + 1) * PER * HD],
                        span_keys[:, head * HD : (head + 1) * HD],
                        span_values[:, head * HD : (head + 1) * HD],
                    ],
                    axis=1,
                )
            )
        packed = jnp.stack(pieces)
        received.append(
            lax.all_to_all(packed, "head", split_axis=0, concat_axis=0, tiled=True).reshape(
                span, (PER + 2) * HD
            )
        )
        mine = jnp.stack([prompt_keys[:, :, c, :], prompt_values[:, :, c, :]])
        every = lax.all_gather(mine, "seq", axis=2, tiled=True)
        prompts.append(lax.dynamic_index_in_dim(every, group, 1, keepdims=False))
    cache_len = prompts[0].shape[1]

    positions = (length + jnp.arange(span, dtype=jnp.int32)).astype(jnp.float32)
    inv_freq = jnp.exp(
        -(jnp.arange(HD // 2, dtype=jnp.float32) * (2.0 / HD)) * math.log(1000000.0)
    )
    angles = positions[:, None] * inv_freq[None, :]
    cos_half, sin_half = jnp.cos(angles), jnp.sin(angles)
    cosine = jnp.concatenate([cos_half, cos_half], axis=1)
    sine = jnp.concatenate([-sin_half, sin_half], axis=1)

    keys, back = [], []
    for c in range(kvl):
        out, key = attend(
            c * PER,
            scalars,
            received[c],
            prompts[c],
            gates,
            query_gain[None],
            key_gain[None],
            cosine,
            sine,
        )
        keys.append(key)
        back.append(
            lax.all_to_all(
                out.reshape(n, rows, PER * HD), "head", split_axis=0, concat_axis=0, tiled=True
            )
        )
    attended = jnp.concatenate([back[c][d] for d in range(n) for c in range(kvl)], axis=1)
    vcol = (PER + 1) * HD
    new_keys = append_span(
        jnp.concatenate([p[0] for p in prompts], axis=1), jnp.concatenate(keys, axis=1), length
    )
    new_values = append_span(
        jnp.concatenate([p[1] for p in prompts], axis=1),
        jnp.concatenate([r[:, vcol:] for r in received], axis=1),
        length,
    )
    shape = (1, cache_len + span, kvl, HD)
    return (attended, new_keys.reshape(shape), new_values.reshape(shape))


def solution(mesh):
    token = P(("seq", "head"), None)
    prompt = P(None, "seq", "head", None)
    cache = P("seq", None, "head", None)
    return jax.shard_map(
        on_device,
        mesh=mesh,
        in_specs=(token, token, token, token, P(), P(), prompt, prompt, P(), P()),
        out_specs=(token, cache, cache),
        check_vma=False,
    )
```

time: 661 us -> 351 us (0.53)
  matrix products: 193 us -> 0 us
  Pallas kernels: 0 us -> 94.1 us
  loops' own time: 89.2 us -> 0 us
  other arithmetic: 112 us -> 25.1 us
  local copies, waits for them, and re-layouts: 161 us -> 84.4 us
  blocking collectives: 0 us -> 25.4 us
  waiting for transfers between devices: 56.1 us -> 66.5 us
  starting transfers between devices: 24.2 us -> 33.9 us
    dot_general x64 -> x0, matrix products: 193 us -> none  [the longest x32 97.2 us: one_block(): lax.dot_general(query_block, key_head, (((1,), (1,)), ((), ())), preferre...]
    pallas_call x0 -> x4, Pallas kernels: none -> 94.1 us  [attend(): pl.pallas_call(functools.partial(attend_kernel, first_head), out_shape=(j...]
    another operation x1 -> x0, loops' own time: 89.2 us -> none  [attend(): lax.map(one_block, jnp.arange(kv_count * per_kv * blocks, dtype=jnp.int32))]
    reduce_sum x34 -> x0, other arithmetic: 39 us -> none  [the longest x32 31.9 us: one_block(): jnp.sum(raised, axis=-1, keepdims=True)]
    convert_element_type x3 -> x0, local copies, waits for them, and re-layouts: 25.6 us -> none  [norm_rope(): upcast = values_in.astype(jnp.float32)]
    all_gather x0 -> x1, blocking collectives: none -> 25.4 us  [on_device(): gates = lax.all_gather(head_gates, 'head', axis=0, tiled=True)]
    dynamic_slice x37 -> x1, local copies, waits for them, and re-layouts: 25.8 us -> 0.59 us  [on_device(): lax.dynamic_index_in_dim(request_group, lax.axis_index('seq'), 0, keepdim...]
    lt x32 -> x0, other arithmetic: 18.4 us -> none  [one_block(): key_pos[None, :] < length]
  transfers between devices with their start and end apart: 7 -> 12, of which waited for: 3 -> 4; matrix products, arithmetic and copies ran while one was open for 23% -> 26% of each run, Pallas kernels for 0% -> 27%
where the time goes in v1:
time: 351 us; the launch traced here: 348 us
  Pallas kernels  94.1 us (27%)
  local copies, waits for them, and re-layouts  84.4 us (24%)
  waiting for transfers between devices  66.5 us (19%)
  starting transfers between devices  33.9 us (10%)
  blocking collectives  25.4 us (7%)
  other arithmetic  25.1 us (7%)
  between operations  18.4 us (5%)
    pallas_call x4, Pallas kernels, attend(): pl.pallas_call(functools.partial(attend_kernel, first_head), out_shape=(j...  94.1 us
    all_to_all x4, waiting for transfers between devices, on_device(): lax.all_to_all(packed, 'head', split_axis=0, concat_axis=0, tiled=True)  59.6 us
    all_gather x1, blocking collectives, on_device(): gates = lax.all_gather(head_gates, 'head', axis=0, tiled=True)  25.4 us
    dynamic_update_slice x2, local copies, waits for them, and re-layouts, append_span(): return lax.dynamic_update_slice_in_dim(base, span_rows, length, 0)  20.9 us
    unnamed x62, local copies, waits for them, and re-layouts  18.2 us
    all_to_all x4, starting transfers between devices, on_device(): lax.all_to_all(packed, 'head', split_axis=0, concat_axis=0, tiled=True)  17.6 us
    all_to_all x4, starting transfers between devices, on_device(): lax.all_to_all(out.reshape(n, rows, PER * HD), 'head', split_axis=0, conc...  16.1 us
    reshape x2, local copies, waits for them, and re-layouts, on_device(): return (attended, new_keys.reshape(shape), new_values.reshape(shape))  11.1 us
  transfers between devices with their start and end apart: 12, of which 4 were waited for; matrix products, arithmetic and copies ran while one was open for 26% of the time, Pallas kernels for 27%

profile of v1, /device:TPU:0, one launch (start us, length us, event | category | flops | bytes accessed | tf_op | source)
XLA Modules:
  0.0 347.7 jit_solution(12187370463557832795)
XLA Ops:
  7.2 2.1 fusion.12
  9.3 2.0 fusion.13
  12.8 2.8 fusion.10
  21.5 4.2 %all-to-all-start.6 = ((bf16[2,1024,512]{2,1,0:T(8,128)(2,1)}), bf16[2,1024,512]{2,1,0:T(8,128)(2,1)S(1)}, u32[]{:S(2)}, u32[]{:S(2)}) async-start(bf16[2,1024,512]{2,1,0:T(8,128)(2,1)} %pad_maximum_fusion.3), calls=%async_computation.6 | async-start | bytes 4194304 | tf_op jit(solution)/shard_map/all_to_all | solution.py:173
  30.5 21.1 %all-to-all-done.6 = bf16[2,1024,512]{2,1,0:T(8,128)(2,1)S(1)} async-done(((bf16[2,1024,512]{2,1,0:T(8,128)(2,1)}), bf16[2,1024,512]{2,1,0:T(8,128)(2,1)S(1)}, u32[]{:S(2)}, u32[]{:S(2)}) %all-to-all-start.6) | async-done | bytes 2097184 | tf_op jit(solution)/shard_map/all_to_all | solution.py:173
  52.9 4.8 %all-to-all-start.4 = ((bf16[2,1024,512]{2,1,0:T(8,128)(2,1)}), bf16[2,1024,512]{2,1,0:T(8,128)(2,1)}, u32[]{:S(2)}, u32[]{:S(2)}) async-start(bf16[2,1024,512]{2,1,0:T(8,128)(2,1)} %pad_maximum_fusion.2), calls=%async_computation.4 | async-start | bytes 4194304 | tf_op jit(solution)/shard_map/all_to_all | solution.py:173
  60.9 21.5 %all-to-all-done.4 = bf16[2,1024,512]{2,1,0:T(8,128)(2,1)} async-done(((bf16[2,1024,512]{2,1,0:T(8,128)(2,1)}), bf16[2,1024,512]{2,1,0:T(8,128)(2,1)}, u32[]{:S(2)}, u32[]{:S(2)}) %all-to-all-start.4) | async-done | bytes 2097184 | tf_op jit(solution)/shard_map/all_to_all | solution.py:173
  82.5 3.8 %all-to-all-start.2 = ((bf16[2,1024,512]{2,1,0:T(8,128)(2,1)}), bf16[2,1024,512]{2,1,0:T(8,128)(2,1)S(1)}, u32[]{:S(2)}, u32[]{:S(2)}) async-start(bf16[2,1024,512]{2,1,0:T(8,128)(2,1)} %pad_maximum_fusion.1), calls=%async_computation.2 | async-start | bytes 4194304 | tf_op jit(solution)/shard_map/all_to_all | solution.py:173
  93.0 17.0 %all-to-all-done.2 = bf16[2,1024,512]{2,1,0:T(8,128)(2,1)S(1)} async-done(((bf16[2,1024,512]{2,1,0:T(8,128)(2,1)}), bf16[2,1024,512]{2,1,0:T(8,128)(2,1)S(1)}, u32[]{:S(2)}, u32[]{:S(2)}) %all-to-all-start.2) | async-done | bytes 2097184 | tf_op jit(solution)/shard_map/all_to_all | solution.py:173
  111.3 4.8 %all-to-all-start = ((bf16[2,1024,512]{2,1,0:T(8,128)(2,1)}), bf16[2,1024,512]{2,1,0:T(8,128)(2,1)}, u32[]{:S(2)}, u32[]{:S(2)}) async-start(bf16[2,1024,512]{2,1,0:T(8,128)(2,1)} %pad_maximum_fusion), calls=%async_computation | async-start | bytes 4194304 | tf_op jit(solution)/shard_map/all_to_all | solution.py:173
  119.1 25.4 %all_gather.16.gate_ref = bf16[2048,16]{1,0:T(8,128)(2,1)S(1)} all-gather(bf16[1024,16]{1,0:T(8,128)(2,1)S(1)} %copy.23), channel_id=1, replica_groups=mesh['seq'=16,'head'=2] {'head'}, dimensions={0}, use_global_device_ids=true | all-gather | bytes 98304 | tf_op jit(solution)/shard_map/all_gather | solution.py:155
  145.9 3.7 %fusion.8 = (f32[2048,64]{1,0:T(8,128)S(1)}, f32[2048,64]{1,0:T(8,128)S(1)}, f32[2048,64]{1,0:T(8,128)S(1)}) fusion(f32[64]{0:T(128)S(1)} %multiply_exponential_fusion, f32[2048]{0:T(1024)S(1)} %add_convert_fusion), kind=kLoop, calls=%fused_computation.40 | loop fusion | flops 262144 | bytes 1581312 | tf_op jit(solution)/shard_map/neg | solution.py:189
  151.3 1.9 slice.226
  153.3 1.9 slice.225
  156.4 2.8 pad_maximum_fusion.5
  160.2 32.1 %shard_map.123 = (bf16[2048,256]{1,0:T(8,128)(2,1)}, bf16[2048,128]{1,0:T(8,128)(2,1)S(1)}) custom-call(s32[2]{0:T(128)S(1)} %pad_add_fusion.length_ref, bf16[2048,512]{1,0:T(8,128)(2,1)} %bitcast.23.rows_ref, bf16[2,1024,128]{2,1,0:T(8,128)(2,1)S(1)} %dynamic-slice_bitcast_fusion.1.prompt_ref, bf16[2048,16]{1,0:T(8,128)(2,1)S(1)} %all_gather.16.gate_ref, ...), custom_call_target="tpu_custom_call" | custom-call | flops 8589934592 | bytes 6291456 | tf_op jit(solution)/shard_map/pallas_call | solution.py:111
  193.2 4.4 %all-to-all-start.5 = ((bf16[2,1024,256]{2,1,0:T(8,128)(2,1)}), bf16[2,1024,256]{2,1,0:T(8,128)(2,1)}, u32[]{:S(2)}, u32[]{:S(2)}) async-start(bf16[2,1024,256]{2,1,0:T(8,128)(2,1)} %bitcast.27), calls=%async_computation.5 | async-start | bytes 2097152 | tf_op jit(solution)/shard_map/all_to_all | solution.py:206
  201.4 1.9 dynamic-slice_bitcast_fusion.2.prompt_ref
  205.2 20.9 %shard_map.124 = (bf16[2048,256]{1,0:T(8,128)(2,1)}, bf16[2048,128]{1,0:T(8,128)(2,1)S(1)}) custom-call(s32[2]{0:T(128)S(1)} %pad_add_fusion.length_ref, bf16[2048,512]{1,0:T(8,128)(2,1)} %bitcast.110, bf16[2,1024,128]{2,1,0:T(8,128)(2,1)S(1)} %dynamic-slice_bitcast_fusion.prompt_ref, bf16[2048,16]{1,0:T(8,128)(2,1)S(1)} %all_gather.16.gate_ref, ...), custom_call_target="tpu_custom_call" | custom-call | flops 8589934592 | bytes 6291456 | tf_op jit(solution)/shard_map/pallas_call | solution.py:111
  226.9 1.9 dynamic-slice_bitcast_fusion.7
  229.9 20.3 %shard_map.122 = (bf16[2048,256]{1,0:T(8,128)(2,1)}, bf16[2048,128]{1,0:T(8,128)(2,1)S(1)}) custom-call(s32[2]{0:T(128)S(1)} %pad_add_fusion.length_ref, bf16[2048,512]{1,0:T(8,128)(2,1)} %bitcast.112, bf16[2,1024,128]{2,1,0:T(8,128)(2,1)S(1)} %copy-done, bf16[2048,16]{1,0:T(8,128)(2,1)S(1)} %all_gather.16.gate_ref, f32[1,128]{1,0:T(1,128)S(1)} %bitcast.103, ...), custom_call_target="tpu_custom_call" | custom-call | flops 8589934592 | bytes 6291456 | tf_op jit(solution)/shard_map/pallas_call | solution.py:111
  251.1 4.4 %all-to-all-start.3 = ((bf16[2,1024,256]{2,1,0:T(8,128)(2,1)}), bf16[2,1024,256]{2,1,0:T(8,128)(2,1)}, u32[]{:S(2)}, u32[]{:S(2)}) async-start(bf16[2,1024,256]{2,1,0:T(8,128)(2,1)} %bitcast.19), calls=%async_computation.3 | async-start | bytes 2097152 | tf_op jit(solution)/shard_map/all_to_all | solution.py:206
  255.5 20.7 %shard_map.121 = (bf16[2048,256]{1,0:T(8,128)(2,1)}, bf16[2048,128]{1,0:T(8,128)(2,1)S(1)}) custom-call(s32[2]{0:T(128)S(1)} %pad_add_fusion.length_ref, bf16[2048,512]{1,0:T(8,128)(2,1)} %bitcast.4.rows_ref, bf16[2,1024,128]{2,1,0:T(8,128)(2,1)S(1)} %dynamic-slice_bitcast_fusion.3.prompt_ref, bf16[2048,16]{1,0:T(8,128)(2,1)S(1)} %all_gather.16.gate_ref, ...), custom_call_target="tpu_custom_call" | custom-call | flops 8589934592 | bytes 6291456 | tf_op jit(solution)/shard_map/pallas_call | solution.py:111
  277.1 3.7 %all-to-all-start.1 = ((bf16[2,1024,256]{2,1,0:T(8,128)(2,1)}), bf16[2,1024,256]{2,1,0:T(8,128)(2,1)S(1)}, u32[]{:S(2)}, u32[]{:S(2)}) async-start(bf16[2,1024,256]{2,1,0:T(8,128)(2,1)} %bitcast.11), calls=%async_computation.1 | async-start | bytes 2097152 | tf_op jit(solution)/shard_map/all_to_all | solution.py:206
  281.7 1.9 concatenate.66
  286.2 10.2 %dynamic_update_slice.7 = bf16[3072,512]{1,0:T(8,128)(2,1)} dynamic-update-slice(bf16[3072,512]{1,0:T(8,128)(2,1)} %concatenate.66, bf16[2048,512]{1,0:T(8,128)(2,1)S(1)} %copy-done.11, s32[]{:T(128)S(6)} %select_n.27, s32[]{:T(128)} %constant.33.clone.1) | dynamic-update-slice | bytes 4194308 | tf_op jit(solution)/shard_map/dynamic_update_slice | solution.py:131
  296.4 5.6 %reshape.77 = bf16[1,3072,4,128]{3,2,1,0:T(4,128)(2,1)} reshape(bf16[3072,512]{1,0:T(8,128)(2,1)} %dynamic_update_slice.7) | data formatting | bytes 6291456 | tf_op jit(solution)/shard_map/reshape | solution.py:221
  303.6 10.7 %dynamic_update_slice.6 = bf16[3072,512]{1,0:T(8,128)(2,1)} dynamic-update-slice(bf16[3072,512]{1,0:T(8,128)(2,1)} %concatenate.63, bf16[2048,512]{1,0:T(8,128)(2,1)} %pad_maximum_fusion.4, s32[]{:T(128)S(6)} %select_n.27, s32[]{:T(128)} %constant.33.clone.1) | dynamic-update-slice | bytes 4194308 | tf_op jit(solution)/shard_map/dynamic_update_slice | solution.py:131
  314.4 5.5 %reshape.76 = bf16[1,3072,4,128]{3,2,1,0:T(4,128)(2,1)} reshape(bf16[3072,512]{1,0:T(8,128)(2,1)} %dynamic_update_slice.6) | data formatting | bytes 6291456 | tf_op jit(solution)/shard_map/reshape | solution.py:221
  319.9 3.6 %all-to-all-start.7 = ((bf16[2,1024,256]{2,1,0:T(8,128)(2,1)}), bf16[2,1024,256]{2,1,0:T(8,128)(2,1)S(1)}, u32[]{:S(2)}, u32[]{:S(2)}) async-start(bf16[2,1024,256]{2,1,0:T(8,128)(2,1)} %bitcast.35), calls=%async_computation.7 | async-start | bytes 2097152 | tf_op jit(solution)/shard_map/all_to_all | solution.py:206
  324.3 1.9 fusion.6
  328.0 6.7 %all-to-all-done.7 = bf16[2,1024,256]{2,1,0:T(8,128)(2,1)S(1)} async-done(((bf16[2,1024,256]{2,1,0:T(8,128)(2,1)}), bf16[2,1024,256]{2,1,0:T(8,128)(2,1)S(1)}, u32[]{:S(2)}, u32[]{:S(2)}) %all-to-all-start.7) | async-done | bytes 1048608 | tf_op jit(solution)/shard_map/all_to_all | solution.py:206
  (114 shorter events, 53.0 us)
Async XLA Ops:
  7.2 152.0 %all-gather.9.cloned.1.call-start = ((), (), s32[]{:S(2)}) async-start(), calls=%async_computation.10 | async-start | bytes 1114112 | tf_op jit(solution)/shard_map/all_gather | solution.py:178
  12.0 185.6 %all-gather.11.cloned.1.call-start = ((), (), s32[]{:S(2)}) async-start(), calls=%async_computation.11 | async-start | bytes 1114112 | tf_op jit(solution)/shard_map/all_gather | solution.py:178
  12.8 2.8 copy-start.15
  15.6 2.8 copy-start.12
  21.5 30.1 %all-to-all-start.6 = ((bf16[2,1024,512]{2,1,0:T(8,128)(2,1)}), bf16[2,1024,512]{2,1,0:T(8,128)(2,1)S(1)}, u32[]{:S(2)}, u32[]{:S(2)}) async-start(bf16[2,1024,512]{2,1,0:T(8,128)(2,1)} %pad_maximum_fusion.3), calls=%async_computation.6 | async-start | bytes 4194304 | tf_op jit(solution)/shard_map/all_to_all | solution.py:173
  25.7 175.7 %all-gather.7.cloned.1.call-start = ((), (), s32[]{:S(2)}) async-start(), calls=%async_computation.9 | async-start | bytes 1114112 | tf_op jit(solution)/shard_map/all_gather | solution.py:178
  52.9 29.6 %all-to-all-start.4 = ((bf16[2,1024,512]{2,1,0:T(8,128)(2,1)}), bf16[2,1024,512]{2,1,0:T(8,128)(2,1)}, u32[]{:S(2)}, u32[]{:S(2)}) async-start(bf16[2,1024,512]{2,1,0:T(8,128)(2,1)} %pad_maximum_fusion.2), calls=%async_computation.4 | async-start | bytes 4194304 | tf_op jit(solution)/shard_map/all_to_all | solution.py:173
  60.9 26.1 %copy-start.25 = (s32[16]{0:T(128)S(1)}, s32[16]{0:T(128)}, u32[]{:S(2)}) copy-start(s32[16]{0:T(128)} %param.19) | copy-start | bytes 196
  60.9 28.6 %copy-start.26 = (s32[2]{0:T(128)S(1)}, s32[2]{0:T(128)}, u32[]{:S(2)}) copy-start(s32[2]{0:T(128)} %param.18) | copy-start | bytes 28
  82.5 27.5 %all-to-all-start.2 = ((bf16[2,1024,512]{2,1,0:T(8,128)(2,1)}), bf16[2,1024,512]{2,1,0:T(8,128)(2,1)S(1)}, u32[]{:S(2)}, u32[]{:S(2)}) async-start(bf16[2,1024,512]{2,1,0:T(8,128)(2,1)} %pad_maximum_fusion.1), calls=%async_computation.2 | async-start | bytes 4194304 | tf_op jit(solution)/shard_map/all_to_all | solution.py:173
  86.2 140.7 %all-gather.5.cloned.1.call-start = ((), (), s32[]{:S(2)}) async-start(), calls=%async_computation.8 | async-start | bytes 1114112 | tf_op jit(solution)/shard_map/all_gather | solution.py:178
  93.0 25.2 %copy-start.24 = (bf16[1024,16]{0,1:T(8,128)(2,1)S(1)}, bf16[1024,16]{0,1:T(8,128)(2,1)}, u32[]{:S(2)}) copy-start(bf16[1024,16]{0,1:T(8,128)(2,1)} %param.13) | copy-start | bytes 98308
  111.3 43.9 %all-to-all-start = ((bf16[2,1024,512]{2,1,0:T(8,128)(2,1)}), bf16[2,1024,512]{2,1,0:T(8,128)(2,1)}, u32[]{:S(2)}, u32[]{:S(2)}) async-start(bf16[2,1024,512]{2,1,0:T(8,128)(2,1)} %pad_maximum_fusion), calls=%async_computation | async-start | bytes 4194304 | tf_op jit(solution)/shard_map/all_to_all | solution.py:173
  156.3 3.9 %copy-start.9 = (f32[128]{0:T(128)S(1)}, f32[128]{0:T(128)}, u32[]{:S(2)}) copy-start(f32[128]{0:T(128)} %param.14) | copy-start | bytes 1540
  156.4 3.9 %copy-start.10 = (f32[128]{0:T(128)S(1)}, f32[128]{0:T(128)}, u32[]{:S(2)}) copy-start(f32[128]{0:T(128)} %param.15) | copy-start | bytes 1540
  193.2 57.9 %all-to-all-start.5 = ((bf16[2,1024,256]{2,1,0:T(8,128)(2,1)}), bf16[2,1024,256]{2,1,0:T(8,128)(2,1)}, u32[]{:S(2)}, u32[]{:S(2)}) async-start(bf16[2,1024,256]{2,1,0:T(8,128)(2,1)} %bitcast.27), calls=%async_computation.5 | async-start | bytes 2097152 | tf_op jit(solution)/shard_map/all_to_all | solution.py:206
  197.6 3.0 copy-start.23
  226.9 3.0 copy-start
  251.1 26.0 %all-to-all-start.3 = ((bf16[2,1024,256]{2,1,0:T(8,128)(2,1)}), bf16[2,1024,256]{2,1,0:T(8,128)(2,1)}, u32[]{:S(2)}, u32[]{:S(2)}) async-start(bf16[2,1024,256]{2,1,0:T(8,128)(2,1)} %bitcast.19), calls=%async_computation.3 | async-start | bytes 2097152 | tf_op jit(solution)/shard_map/all_to_all | solution.py:206
  277.0 3.8 %copy-start.16 = (bf16[1024,128]{1,0:T(8,128)(2,1)S(1)}, bf16[1024,128]{1,0:T(8,128)(2,1)}, u32[]{:S(2)}) copy-start(bf16[1024,128]{1,0:T(8,128)(2,1)} %get-tuple-element.50) | copy-start | bytes 786436
  277.0 3.8 %copy-start.17 = (bf16[1024,128]{1,0:T(8,128)(2,1)S(1)}, bf16[1024,128]{1,0:T(8,128)(2,1)}, u32[]{:S(2)}) copy-start(bf16[1024,128]{1,0:T(8,128)(2,1)} %get-tuple-element.47) | copy-start | bytes 786436
  277.0 3.8 %copy-start.18 = (bf16[1024,128]{1,0:T(8,128)(2,1)S(1)}, bf16[1024,128]{1,0:T(8,128)(2,1)}, u32[]{:S(2)}) copy-start(bf16[1024,128]{1,0:T(8,128)(2,1)} %get-tuple-element.48) | copy-start | bytes 786436
  277.0 3.8 %copy-start.19 = (bf16[1024,128]{1,0:T(8,128)(2,1)S(1)}, bf16[1024,128]{1,0:T(8,128)(2,1)}, u32[]{:S(2)}) copy-start(bf16[1024,128]{1,0:T(8,128)(2,1)} %get-tuple-element.45) | copy-start | bytes 786436
  277.0 3.8 %copy-start.20 = (bf16[1024,128]{1,0:T(8,128)(2,1)S(1)}, bf16[1024,128]{1,0:T(8,128)(2,1)}, u32[]{:S(2)}) copy-start(bf16[1024,128]{1,0:T(8,128)(2,1)} %get-tuple-element.46) | copy-start | bytes 786436
  277.0 3.8 %copy-start.21 = (bf16[1024,128]{1,0:T(8,128)(2,1)S(1)}, bf16[1024,128]{1,0:T(8,128)(2,1)}, u32[]{:S(2)}) copy-start(bf16[1024,128]{1,0:T(8,128)(2,1)} %get-tuple-element.43) | copy-start | bytes 786436
  277.0 3.8 %copy-start.22 = (bf16[1024,128]{1,0:T(8,128)(2,1)S(1)}, bf16[1024,128]{1,0:T(8,128)(2,1)}, u32[]{:S(2)}) copy-start(bf16[1024,128]{1,0:T(8,128)(2,1)} %get-tuple-element.44) | copy-start | bytes 786436
  277.1 42.8 %all-to-all-start.1 = ((bf16[2,1024,256]{2,1,0:T(8,128)(2,1)}), bf16[2,1024,256]{2,1,0:T(8,128)(2,1)S(1)}, u32[]{:S(2)}, u32[]{:S(2)}) async-start(bf16[2,1024,256]{2,1,0:T(8,128)(2,1)} %bitcast.11), calls=%async_computation.1 | async-start | bytes 2097152 | tf_op jit(solution)/shard_map/all_to_all | solution.py:206
  296.4 5.7 %copy-start.2 = (bf16[2048,128]{1,0:T(8,128)(2,1)S(1)}, bf16[2048,128]{1,0:T(8,128)(2,1)}, u32[]{:S(2)}) copy-start(bf16[2048,128]{1,0:T(8,128)(2,1)} %copy-done.1) | copy-start | bytes 1572868
  296.4 5.7 %copy-start.4 = (bf16[2048,128]{1,0:T(8,128)(2,1)S(1)}, bf16[2048,128]{1,0:T(8,128)(2,1)}, u32[]{:S(2)}) copy-start(bf16[2048,128]{1,0:T(8,128)(2,1)} %copy-done.3) | copy-start | bytes 1572868
  296.4 5.7 %copy-start.6 = (bf16[2048,128]{1,0:T(8,128)(2,1)S(1)}, bf16[2048,128]{1,0:T(8,128)(2,1)}, u32[]{:S(2)}) copy-start(bf16[2048,128]{1,0:T(8,128)(2,1)} %copy-done.5) | copy-start | bytes 1572868
  296.4 5.7 %copy-start.8 = (bf16[2048,128]{1,0:T(8,128)(2,1)S(1)}, bf16[2048,128]{1,0:T(8,128)(2,1)}, u32[]{:S(2)}) copy-start(bf16[2048,128]{1,0:T(8,128)(2,1)} %copy-done.7) | copy-start | bytes 1572868
  319.9 14.9 %all-to-all-start.7 = ((bf16[2,1024,256]{2,1,0:T(8,128)(2,1)}), bf16[2,1024,256]{2,1,0:T(8,128)(2,1)S(1)}, u32[]{:S(2)}, u32[]{:S(2)}) async-start(bf16[2,1024,256]{2,1,0:T(8,128)(2,1)} %bitcast.35), calls=%async_computation.7 | async-start | bytes 2097152 | tf_op jit(solution)/shard_map/all_to_all | solution.py:206
  (7 other events, 8.5 us)
Sparse Core Ops, SparseCore 0:
  12.1 40.6 all-gather.8
  55.0 36.8 all-gather.10
  94.1 36.8 all-gather.6
  133.0 36.9 all-gather.4

commit v2 on v1

--- a/solution.py
+++ b/solution.py
@@ -24,7 +24,6 @@
 
 
 def attend_kernel(
-    first_head,
     length_ref,
     rows_ref,
     prompt_ref,
@@ -35,11 +34,13 @@
     sin_ref,
     out_ref,
     key_ref,
+    token_ref,
 ):
+    token_ref[0] = length_ref[2]
     span = rows_ref.shape[0]
     cache_len = prompt_ref.shape[1]
     length = length_ref[0]
-    head0 = length_ref[1] + first_head
+    head0 = length_ref[1]
     bq = min(BQ, span)
     blocks = span // bq
     const = LOG2E / math.sqrt(HD)
@@ -103,19 +104,20 @@
             finish(*item)
 
 
-def attend(first_head, scalars, rows, prompt, gates, qgain, kgain, cosine, sine):
+def attend(scalars, rows, prompt, gates, qgain, kgain, cosine, sine):
     span = rows.shape[0]
     cache_len = prompt.shape[1]
     vmem = pl.BlockSpec(memory_space=pltpu.VMEM)
     pairs = PER * span * (cache_len + span // 2)
     return pl.pallas_call(
-        functools.partial(attend_kernel, first_head),
+        attend_kernel,
         out_shape=(
             jax.ShapeDtypeStruct((span, PER * HD), jnp.bfloat16),
             jax.ShapeDtypeStruct((span, HD), jnp.bfloat16),
+            jax.ShapeDtypeStruct((1,), jnp.int32),
         ),
         in_specs=[pl.BlockSpec(memory_space=pltpu.SMEM)] + [vmem] * 7,
-        out_specs=(vmem, vmem),
+        out_specs=(vmem, vmem, pl.BlockSpec(memory_space=pltpu.SMEM)),
         compiler_params=pltpu.CompilerParams(vmem_limit_bytes=48 * 1024 * 1024),
         cost_estimate=pl.CostEstimate(
             flops=8 * pairs * HD, bytes_accessed=6 * span * HD * 4, transcendentals=pairs
@@ -126,7 +128,7 @@
 def append_span(prefix, span_rows, length):
     cache_len = prefix.shape[0]
     slot_pos = jnp.arange(cache_len, dtype=jnp.int32)
-    kept = jnp.where((slot_pos < length)[:, None], prefix, jnp.zeros_like(prefix))
+    kept = jnp.where((slot_pos < length)[:, None, None], prefix, jnp.zeros_like(prefix))
     base = jnp.concatenate([kept, jnp.zeros_like(span_rows)], axis=0)
     return lax.dynamic_update_slice_in_dim(base, span_rows, length, 0)
 
@@ -150,34 +152,37 @@
     groups, part, _, _ = prompt_keys.shape
     group = lax.dynamic_index_in_dim(request_group, lax.axis_index("seq"), 0, keepdims=False)
     length = lax.dynamic_index_in_dim(prompt_length, group, 0, keepdims=False)
-    scalars = jnp.stack([length, lax.axis_index("head") * (kvl * PER)]).astype(jnp.int32)
-
-    gates = lax.all_gather(head_gates, "head", axis=0, tiled=True)
-    received, prompts = [], []
-    for c in range(kvl):
-        pieces = []
-        for d in range(n):
+    gates = lax.all_to_all(
+        head_gates.T.reshape(n, kvl * PER, rows), "head", split_axis=0, concat_axis=0, tiled=True
+    )
+    gates = gates.transpose(0, 2, 1).reshape(span, kvl * PER)
+
+    step = max(1, kvl // 2)
+    gathered = []
+    for c in range(0, kvl, step):
+        mine = jnp.stack(
+            [
+                jnp.stack([p[:, :, c + k, :] for k in range(step)])
+                for p in (prompt_keys, prompt_values)
+            ],
+            axis=1,
+        )
+        gathered.append(lax.all_gather(mine, "seq", axis=3, tiled=True))
+    cache_len = gathered[0].shape[3]
+
+    def send(pieces):
+        return lax.all_to_all(pieces, "head", split_axis=0, concat_axis=0, tiled=True)
+
+    def pack(c):
+        def part(d):
             head = d * kvl + c
-            pieces.append(
-                jnp.concatenate(
-                    [
-                        queries[:, head * PER * HD : (head + 1) * PER * HD],
-                        span_keys[:, head * HD : (head + 1) * HD],
-                        span_values[:, head * HD : (head + 1) * HD],
-                    ],
-                    axis=1,
-                )
-            )
-        packed = jnp.stack(pieces)
-        received.append(
-            lax.all_to_all(packed, "head", split_axis=0, concat_axis=0, tiled=True).reshape(
-                span, (PER + 2) * HD
-            )
-        )
-        mine = jnp.stack([prompt_keys[:, :, c, :], prompt_values[:, :, c, :]])
-        every = lax.all_gather(mine, "seq", axis=2, tiled=True)
-        prompts.append(lax.dynamic_index_in_dim(every, group, 1, keepdims=False))
-    cache_len = prompts[0].shape[1]
+            return [
+                queries[:, head * PER * HD : (head + 1) * PER * HD],
+                span_keys[:, head * HD : (head + 1) * HD],
+                span_values[:, head * HD : (head + 1) * HD],
+            ]
+
+        return jnp.stack([jnp.concatenate(part(d), axis=1) for d in range(n)])
 
     positions = (length + jnp.arange(span, dtype=jnp.int32)).astype(jnp.float32)
     inv_freq = jnp.exp(
@@ -188,11 +193,19 @@
     cosine = jnp.concatenate([cos_half, cos_half], axis=1)
     sine = jnp.concatenate([-sin_half, sin_half], axis=1)
 
-    keys, back = [], []
+    zero = jnp.int32(0)
+    width = (PER + 2) * HD
+    received = [send(pack(c)).reshape(span, width) for c in range(min(2, kvl))]
+    keys, back, prompts = [], [], []
+    token = zero
     for c in range(kvl):
-        out, key = attend(
-            c * PER,
-            scalars,
+        if c % step == 0:
+            chosen = group + token
+        prompts.append(
+            lax.dynamic_index_in_dim(gathered[c // step][c % step], chosen, 1, keepdims=False)
+        )
+        out, key, mark = attend(
+            jnp.stack([length, jnp.int32(c * PER), zero]),
             received[c],
             prompts[c],
             gates,
@@ -201,24 +214,26 @@
             cosine,
             sine,
         )
+        token = mark[0]
         keys.append(key)
-        back.append(
-            lax.all_to_all(
-                out.reshape(n, rows, PER * HD), "head", split_axis=0, concat_axis=0, tiled=True
-            )
-        )
+        out = out.reshape(n, rows, PER * HD)
+        if c + 2 < kvl:
+            both = send(jnp.concatenate([pack(c + 2), out], axis=2))
+            received.append(both.reshape(span, width + PER * HD))
+            back.append(both[:, :, width:])
+        else:
+            back.append(send(out))
     attended = jnp.concatenate([back[c][d] for d in range(n) for c in range(kvl)], axis=1)
     vcol = (PER + 1) * HD
     new_keys = append_span(
-        jnp.concatenate([p[0] for p in prompts], axis=1), jnp.concatenate(keys, axis=1), length
+        jnp.stack([p[0] for p in prompts], axis=1), jnp.stack(keys, axis=1), length
     )
     new_values = append_span(
-        jnp.concatenate([p[1] for p in prompts], axis=1),
-        jnp.concatenate([r[:, vcol:] for r in received], axis=1),
+        jnp.stack([p[1] for p in prompts], axis=1),
+        jnp.stack([r[:, vcol:width] for r in received], axis=1),
         length,
     )
-    shape = (1, cache_len + span, kvl, HD)
-    return (attended, new_keys.reshape(shape), new_values.reshape(shape))
+    return (attended, new_keys[None], new_values[None])
 
 
 def solution(mesh):

time: 351 us -> 328 us (0.934); the launches traced: 348 us -> 321 us
  blocking collectives: 25.4 us -> 0 us
  local copies, waits for them, and re-layouts: 84.4 us -> 98.9 us
  Pallas kernels: 94.1 us -> 82.3 us
  waiting for transfers between devices: 66.5 us -> 60.9 us
    all_gather x1 -> x0, blocking collectives: 25.4 us -> none  [on_device(): gates = lax.all_gather(head_gates, 'head', axis=0, tiled=True)]
    unnamed x62 -> x105, local copies, waits for them, and re-layouts: 18.2 us -> 43.6 us
    pallas_call x4, Pallas kernels: 94.1 us -> 82.3 us  [attend(): pl.pallas_call(attend_kernel, out_shape=(jax.ShapeDtypeStruct((span, PER...]
    reshape x2 -> x0, local copies, waits for them, and re-layouts: 11.1 us -> none  [on_device(): return (attended, new_keys.reshape(shape), new_values.reshape(shape))]
    another operation x4 -> x10, local copies, waits for them, and re-layouts: 0.92 us -> 10.9 us  [the longest x4 7.74 us: on_device(): jnp.stack([r[:, vcol:width] for r in received], axis=1)]
    squeeze x8 -> x4, local copies, waits for them, and re-layouts: 11.6 us -> 1.76 us  [on_device(): lax.dynamic_index_in_dim(gathered[c // step][c % step], chosen, 1, keepdi...]
    all_to_all x8 -> x7, waiting for transfers between devices: 66.3 us -> 60.9 us  [the longest x6 60.9 us: send(): lax.all_to_all(pieces, 'head', split_axis=0, concat_axis=0, tiled=True)]
    slice x9 -> x7, local copies, waits for them, and re-layouts: 15.9 us -> 11.5 us  [the longest x2 4.37 us: on_device(): gathered[c // step][c % step]]
  transfers between devices with their start and end apart: 12 -> 9, of which waited for: 4 -> 4; matrix products, arithmetic and copies ran while one was open for 26% -> 32% of each run, Pallas kernels for 27% -> 19%
where the time goes in v2:
time: 328 us; the launch traced here: 321 us
  local copies, waits for them, and re-layouts  98.9 us (30%)
  Pallas kernels  82.3 us (25%)
  waiting for transfers between devices  60.9 us (19%)
  starting transfers between devices  33.5 us (10%)
  other arithmetic  25.9 us (8%)
  between operations  19.6 us (6%)
    pallas_call x4, Pallas kernels, attend(): pl.pallas_call(attend_kernel, out_shape=(jax.ShapeDtypeStruct((span, PER...  82.3 us
    all_to_all x6, waiting for transfers between devices, send(): lax.all_to_all(pieces, 'head', split_axis=0, concat_axis=0, tiled=True)  60.9 us
    unnamed x105, local copies, waits for them, and re-layouts  43.6 us
    all_to_all x6, starting transfers between devices, send(): lax.all_to_all(pieces, 'head', split_axis=0, concat_axis=0, tiled=True)  29.2 us
    dynamic_update_slice x2, local copies, waits for them, and re-layouts, append_span(): return lax.dynamic_update_slice_in_dim(base, span_rows, length, 0)  23.8 us
    another operation x6, other arithmetic, pack(): return jnp.stack([jnp.concatenate(part(d), axis=1) for d in range(n)])  7.95 us
    another operation x4, local copies, waits for them, and re-layouts, on_device(): jnp.stack([r[:, vcol:width] for r in received], axis=1)  7.74 us
  transfers between devices with their start and end apart: 9, of which 4 were waited for; matrix products, arithmetic and copies ran while one was open for 32% of the time, Pallas kernels for 19%

profile of v2, /device:TPU:0, one launch (start us, length us, event | category | flops | bytes accessed | tf_op | source)
XLA Modules:
  0.0 321.2 jit_solution(2889645669173583489)
XLA Ops:
  11.0 4.2 %all-to-all-start.1 = ((bf16[2,8,1024]{2,1,0:T(8,128)(2,1)}), bf16[2,8,1024]{2,1,0:T(8,128)(2,1)S(1)}, u32[]{:S(2)}, u32[]{:S(2)}) async-start(bf16[2,8,1024]{2,1,0:T(8,128)(2,1)} %bitcast.14), calls=%async_computation.1 | async-start | bytes 65536 | tf_op jit(solution)/shard_map/all_to_all | solution.py:155
  28.4 4.8 %all-to-all-start = ((bf16[2,1024,512]{2,1,0:T(8,128)(2,1)}), bf16[2,1024,512]{2,1,0:T(8,128)(2,1)}, u32[]{:S(2)}, u32[]{:S(2)}) async-start(bf16[2,1024,512]{2,1,0:T(8,128)(2,1)} %pad_maximum_fusion.2), calls=%async_computation | async-start | bytes 4194304 | tf_op jit(solution)/shard_map/all_to_all | solution.py:174
  38.7 5.5 %fusion.8 = (f32[2048,64]{1,0:T(8,128)S(1)}, f32[2048,64]{1,0:T(8,128)}, f32[2048,64]{1,0:T(8,128)}) fusion(f32[64]{0:T(128)S(1)} %multiply_exponential_fusion, f32[2048]{0:T(1024)S(1)} %add_convert_fusion), kind=kLoop, calls=%fused_computation.46 | loop fusion | flops 262144 | bytes 1581312 | tf_op jit(solution)/shard_map/neg | solution.py:194
  44.2 14.6 %all-to-all-done = bf16[2,1024,512]{2,1,0:T(8,128)(2,1)} async-done(((bf16[2,1024,512]{2,1,0:T(8,128)(2,1)}), bf16[2,1024,512]{2,1,0:T(8,128)(2,1)}, u32[]{:S(2)}, u32[]{:S(2)}) %all-to-all-start) | async-done | bytes 2097184 | tf_op jit(solution)/shard_map/all_to_all | solution.py:174
  58.8 4.9 %all-to-all-start.3 = ((bf16[2,1024,512]{2,1,0:T(8,128)(2,1)}), bf16[2,1024,512]{2,1,0:T(8,128)(2,1)}, u32[]{:S(2)}, u32[]{:S(2)}) async-start(bf16[2,1024,512]{2,1,0:T(8,128)(2,1)} %pad_maximum_fusion.3), calls=%async_computation.3 | async-start | bytes 4194304 | tf_op jit(solution)/shard_map/all_to_all | solution.py:174
  70.4 2.0 slice_bitcast_fusion.3
  72.4 15.9 %all-to-all-done.3 = bf16[2,1024,512]{2,1,0:T(8,128)(2,1)} async-done(((bf16[2,1024,512]{2,1,0:T(8,128)(2,1)}), bf16[2,1024,512]{2,1,0:T(8,128)(2,1)}, u32[]{:S(2)}, u32[]{:S(2)}) %all-to-all-start.3) | async-done | bytes 2097184 | tf_op jit(solution)/shard_map/all_to_all | solution.py:174
  88.3 1.9 slice_bitcast_fusion.2
  90.2 2.7 fusion.13
  93.8 20.4 %shard_map.121 = (bf16[2048,256]{1,0:T(8,128)(2,1)S(1)}, bf16[2048,128]{1,0:T(8,128)(2,1)S(1)}, s32[1]{0:T(128)}) custom-call(s32[3]{0:T(128)S(1)} %stack.121.length_ref, bf16[2048,512]{1,0:T(8,128)(2,1)} %bitcast.5.rows_ref, bf16[2,1024,128]{2,1,0:T(8,128)(2,1)S(1)} %dynamic-slice_bitcast_fusion.3.prompt_ref, bf16[2048,8]{1,0:T(8,128)(2,1)S(1)} %bitcast.140, ...), custom_call_target="tpu_custom_call" | custom-call | flops 8589934592 | bytes 6291456 | tf_op jit(solution)/shard_map/pallas_call | solution.py:112
  115.1 1.9 pad_maximum_fusion
  116.9 5.3 %all-to-all-start.2 = ((bf16[2,1024,768]{2,1,0:T(8,128)(2,1)}), bf16[2,1024,768]{2,1,0:T(8,128)(2,1)}, u32[]{:S(2)}, u32[]{:S(2)}) async-start(bf16[2,1024,768]{2,1,0:T(8,128)(2,1)} %pad_maximum_fusion), calls=%async_computation.2 | async-start | bytes 6291456 | tf_op jit(solution)/shard_map/all_to_all | solution.py:174
  123.4 19.7 %shard_map.122 = (bf16[2048,256]{1,0:T(8,128)(2,1)S(1)}, bf16[2048,128]{1,0:T(8,128)(2,1)S(1)}, s32[1]{0:T(128)}) custom-call(s32[3]{0:T(128)S(1)} %pad_add_fusion.2.length_ref, bf16[2048,512]{1,0:T(8,128)(2,1)} %bitcast.26.rows_ref, bf16[2,1024,128]{2,1,0:T(8,128)(2,1)S(1)} %dynamic-slice_bitcast_fusion.2.prompt_ref, bf16[2048,8]{1,0:T(8,128)(2,1)S(1)} %bitcast.141, ...), custom_call_target="tpu_custom_call" | custom-call | flops 8589934592 | bytes 6291456 | tf_op jit(solution)/shard_map/pallas_call | solution.py:112
  153.0 4.2 %all-to-all-done.2 = bf16[2,1024,768]{2,1,0:T(8,128)(2,1)} async-done(((bf16[2,1024,768]{2,1,0:T(8,128)(2,1)}), bf16[2,1024,768]{2,1,0:T(8,128)(2,1)}, u32[]{:S(2)}, u32[]{:S(2)}) %all-to-all-start.2) | async-done | bytes 3145760 | tf_op jit(solution)/shard_map/all_to_all | solution.py:174
  157.2 5.2 %all-to-all-start.4 = ((bf16[2,1024,768]{2,1,0:T(8,128)(2,1)}), bf16[2,1024,768]{2,1,0:T(8,128)(2,1)}, u32[]{:S(2)}, u32[]{:S(2)}) async-start(bf16[2,1024,768]{2,1,0:T(8,128)(2,1)} %pad_maximum_fusion.1), calls=%async_computation.4 | async-start | bytes 6291456 | tf_op jit(solution)/shard_map/all_to_all | solution.py:174
  164.3 2.0 pad_bitcast_fusion
  166.3 1.9 pad_bitcast_fusion.1
  168.3 2.0 slice_bitcast_fusion.1
  170.2 26.2 %all-to-all-done.4 = bf16[2,1024,768]{2,1,0:T(8,128)(2,1)} async-done(((bf16[2,1024,768]{2,1,0:T(8,128)(2,1)}), bf16[2,1024,768]{2,1,0:T(8,128)(2,1)}, u32[]{:S(2)}, u32[]{:S(2)}) %all-to-all-start.4) | async-done | bytes 3145760 | tf_op jit(solution)/shard_map/all_to_all | solution.py:174
  196.5 1.9 slice_bitcast_fusion
  198.4 21.1 %shard_map.123 = (bf16[2048,256]{1,0:T(8,128)(2,1)}, bf16[2048,128]{1,0:T(8,128)(2,1)S(1)}, s32[1]{0:T(128)}) custom-call(s32[3]{0:T(128)S(1)} %pad_add_fusion.1.length_ref, bf16[2048,768]{1,0:T(8,128)(2,1)} %bitcast.30.rows_ref, bf16[2,1024,128]{2,1,0:T(8,128)(2,1)S(1)} %copy-done.4, bf16[2048,8]{1,0:T(8,128)(2,1)S(1)} %bitcast.142, ...), custom_call_target="tpu_custom_call" | custom-call | flops 8589934592 | bytes 6291456 | tf_op jit(solution)/shard_map/pallas_call | solution.py:112
  220.3 4.6 %all-to-all-start.5 = ((bf16[2,1024,256]{2,1,0:T(8,128)(2,1)}), bf16[2,1024,256]{2,1,0:T(8,128)(2,1)}, u32[]{:S(2)}, u32[]{:S(2)}) async-start(bf16[2,1024,256]{2,1,0:T(8,128)(2,1)} %bitcast.39), calls=%async_computation.5 | async-start | bytes 2097152 | tf_op jit(solution)/shard_map/all_to_all | solution.py:174
  224.9 21.0 %shard_map.124 = (bf16[2048,256]{1,0:T(8,128)(2,1)}, bf16[2048,128]{1,0:T(8,128)(2,1)S(1)}, s32[1]{0:T(128)}) custom-call(s32[3]{0:T(128)S(1)} %pad_add_fusion.length_ref, bf16[2048,768]{1,0:T(8,128)(2,1)} %bitcast.41.rows_ref, bf16[2,1024,128]{2,1,0:T(8,128)(2,1)S(1)} %copy-done.3, bf16[2048,8]{1,0:T(8,128)(2,1)S(1)} %bitcast.143, f32[1,128]{1,0:T(1,128)S(1)} %bitcast.151, ...), custom_call_target="tpu_custom_call" | custom-call | flops 8589934592 | bytes 6291456 | tf_op jit(solution)/shard_map/pallas_call | solution.py:112
  249.0 4.4 %all-to-all-start.6 = ((bf16[2,1024,256]{2,1,0:T(8,128)(2,1)}), bf16[2,1024,256]{2,1,0:T(8,128)(2,1)}, u32[]{:S(2)}, u32[]{:S(2)}) async-start(bf16[2,1024,256]{2,1,0:T(8,128)(2,1)} %bitcast.43), calls=%async_computation.6 | async-start | bytes 2097152 | tf_op jit(solution)/shard_map/all_to_all | solution.py:174
  253.4 1.9 fusion.7
  255.2 12.2 %dynamic_update_slice.9 = bf16[1,3072,4,128]{3,1,2,0:T(8,128)(2,1)} dynamic-update-slice(bf16[1,3072,4,128]{3,1,2,0:T(8,128)(2,1)} %pad_bitcast_fusion, bf16[1,2048,4,128]{3,1,2,0:T(8,128)(2,1)S(1)} %maximum_bitcast_fusion.1, s32[]{:T(128)} %constant.41.clone.1, s32[]{:T(128)S(6)} %select_n.30, s32[]{:T(128)} %constant.41.clone.1, s32[]{:T(128)} %constant.41.clone.1) | dynamic-update-slice | bytes 4194308 | tf_op jit(solution)/shard_map/dynamic_update_slice | solution.py:133
  267.5 6.4 %copy.49 = bf16[1,3072,4,128]{3,2,1,0:T(4,128)(2,1)} copy(bf16[1,3072,4,128]{3,1,2,0:T(8,128)(2,1)} %dynamic_update_slice.9) | data formatting | bytes 6291456
  273.9 11.6 %dynamic_update_slice.8 = bf16[1,3072,4,128]{3,1,2,0:T(8,128)(2,1)S(1)} dynamic-update-slice(bf16[1,3072,4,128]{3,1,2,0:T(8,128)(2,1)S(1)} %copy-done.13, bf16[1,2048,4,128]{3,1,2,0:T(8,128)(2,1)} %maximum_bitcast_fusion, s32[]{:T(128)} %constant.41.clone.1, s32[]{:T(128)S(6)} %select_n.30, s32[]{:T(128)} %constant.41.clone.1, s32[]{:T(128)} %constant.41.clone.1) | dynamic-update-slice | bytes 4194308 | tf_op jit(solution)/shard_map/dynamic_update_slice | solution.py:133
  285.5 15.6 %copy.48 = bf16[1,3072,4,128]{3,2,1,0:T(4,128)(2,1)} copy(bf16[1,3072,4,128]{3,1,2,0:T(8,128)(2,1)S(1)} %dynamic_update_slice.8) | data formatting | bytes 6291456
  304.8 1.9 fusion.4
  308.5 1.9 fusion.2
  310.4 1.9 fusion.1
  (151 shorter events, 49.9 us)
Async XLA Ops:
  7.2 8.9 %copy-start.44 = (s32[16]{0:T(128)S(1)}, s32[16]{0:T(128)}, u32[]{:S(2)}) copy-start(s32[16]{0:T(128)} %param.19) | copy-start | bytes 196
  7.2 11.4 %copy-start.45 = (s32[2]{0:T(128)S(1)}, s32[2]{0:T(128)}, u32[]{:S(2)}) copy-start(s32[2]{0:T(128)} %param.18) | copy-start | bytes 28
  7.2 12.5 %copy-start.25 = (bf16[1024,1024]{1,0:T(8,128)(2,1)S(1)}, bf16[1024,1024]{1,0:T(8,128)(2,1)}, u32[]{:S(2)}) copy-start(bf16[1024,1024]{1,0:T(8,128)(2,1)} %param.11) | copy-start | bytes 6291460
  7.2 83.0 %all-gather.3.cloned.1.call-start = ((), (), s32[]{:S(2)}) async-start(), calls=%async_computation.7 | async-start | bytes 2228224 | tf_op jit(solution)/shard_map/all_gather | solution.py:170
  11.0 17.4 %all-to-all-start.1 = ((bf16[2,8,1024]{2,1,0:T(8,128)(2,1)}), bf16[2,8,1024]{2,1,0:T(8,128)(2,1)S(1)}, u32[]{:S(2)}, u32[]{:S(2)}) async-start(bf16[2,8,1024]{2,1,0:T(8,128)(2,1)} %bitcast.14), calls=%async_computation.1 | async-start | bytes 65536 | tf_op jit(solution)/shard_map/all_to_all | solution.py:155
  15.2 129.9 %all-gather.5.cloned.1.call-start = ((), (), s32[]{:S(2)}) async-start(), calls=%async_computation.8 | async-start | bytes 2228224 | tf_op jit(solution)/shard_map/all_gather | solution.py:170
  28.4 30.4 %all-to-all-start = ((bf16[2,1024,512]{2,1,0:T(8,128)(2,1)}), bf16[2,1024,512]{2,1,0:T(8,128)(2,1)}, u32[]{:S(2)}, u32[]{:S(2)}) async-start(bf16[2,1024,512]{2,1,0:T(8,128)(2,1)} %pad_maximum_fusion.2), calls=%async_computation | async-start | bytes 4194304 | tf_op jit(solution)/shard_map/all_to_all | solution.py:174
  44.2 23.0 %copy-start.27 = (bf16[1024,256]{1,0:T(8,128)(2,1)S(1)}, bf16[1024,256]{1,0:T(8,128)(2,1)}, u32[]{:S(2)}) copy-start(bf16[1024,256]{1,0:T(8,128)(2,1)} %get-tuple-element.31) | copy-start | bytes 1572868
  44.2 23.0 %copy-start.28 = (bf16[1024,256]{1,0:T(8,128)(2,1)S(1)}, bf16[1024,256]{1,0:T(8,128)(2,1)}, u32[]{:S(2)}) copy-start(bf16[1024,256]{1,0:T(8,128)(2,1)} %get-tuple-element.32) | copy-start | bytes 1572868
  44.2 23.0 %copy-start.33 = (bf16[1024,128]{1,0:T(8,128)(2,1)S(1)}, bf16[1024,128]{1,0:T(8,128)(2,1)}, u32[]{:S(2)}) copy-start(bf16[1024,128]{1,0:T(8,128)(2,1)} %get-tuple-element.42) | copy-start | bytes 786436
  44.2 23.0 %copy-start.34 = (bf16[1024,128]{1,0:T(8,128)(2,1)S(1)}, bf16[1024,128]{1,0:T(8,128)(2,1)}, u32[]{:S(2)}) copy-start(bf16[1024,128]{1,0:T(8,128)(2,1)} %get-tuple-element.49) | copy-start | bytes 786436
  44.2 23.0 %copy-start.35 = (bf16[1024,128]{1,0:T(8,128)(2,1)S(1)}, bf16[1024,128]{1,0:T(8,128)(2,1)}, u32[]{:S(2)}) copy-start(bf16[1024,128]{1,0:T(8,128)(2,1)} %get-tuple-element.50) | copy-start | bytes 786436
  58.8 29.5 %all-to-all-start.3 = ((bf16[2,1024,512]{2,1,0:T(8,128)(2,1)}), bf16[2,1024,512]{2,1,0:T(8,128)(2,1)}, u32[]{:S(2)}, u32[]{:S(2)}) async-start(bf16[2,1024,512]{2,1,0:T(8,128)(2,1)} %pad_maximum_fusion.3), calls=%async_computation.3 | async-start | bytes 4194304 | tf_op jit(solution)/shard_map/all_to_all | solution.py:174
  70.4 23.4 %copy-start = (bf16[2,1024,8]{2,1,0:T(8,128)(2,1)}, bf16[2,1024,8]{2,1,0:T(8,128)(2,1)S(1)}, u32[]{:S(2)}) copy-start(bf16[2,1024,8]{2,1,0:T(8,128)(2,1)S(1)} %copy.43) | copy-start | bytes 98308
  93.8 21.2 %copy-start.23 = (bf16[1,1024,512]{2,1,0:T(8,128)(2,1)S(1)}, bf16[1,1024,512]{2,1,0:T(8,128)(2,1)}, u32[]{:S(2)}) copy-start(bf16[1,1024,512]{2,1,0:T(8,128)(2,1)} %get-tuple-element.78) | copy-start | bytes 3145732
  93.8 21.2 %copy-start.24 = (bf16[1,1024,512]{2,1,0:T(8,128)(2,1)S(1)}, bf16[1,1024,512]{2,1,0:T(8,128)(2,1)}, u32[]{:S(2)}) copy-start(bf16[1,1024,512]{2,1,0:T(8,128)(2,1)} %get-tuple-element.79) | copy-start | bytes 3145732
  116.9 5.3 %copy-start.19 = (bf16[1,2,2,1024,128]{4,3,2,1,0:T(8,128)(2,1)S(1)}, bf16[1,2,2,1024,128]{4,3,2,1,0:T(8,128)(2,1)}, u32[]{:S(2)}) copy-start(bf16[1,2,2,1024,128]{4,3,2,1,0:T(8,128)(2,1)} %get-tuple-element.53) | copy-start | bytes 3145732
  116.9 40.3 %all-to-all-start.2 = ((bf16[2,1024,768]{2,1,0:T(8,128)(2,1)}), bf16[2,1024,768]{2,1,0:T(8,128)(2,1)}, u32[]{:S(2)}, u32[]{:S(2)}) async-start(bf16[2,1024,768]{2,1,0:T(8,128)(2,1)} %pad_maximum_fusion), calls=%async_computation.2 | async-start | bytes 6291456 | tf_op jit(solution)/shard_map/all_to_all | solution.py:174
  153.0 9.5 %copy-start.40 = (bf16[1024,1,128]{2,0,1:T(8,128)(2,1)S(1)}, bf16[1024,1,128]{2,0,1:T(8,128)(2,1)}, u32[]{:S(2)}) copy-start(bf16[1024,1,128]{2,0,1:T(8,128)(2,1)} %get-tuple-element.62) | copy-start | bytes 786436
  153.0 9.5 %copy-start.41 = (bf16[1024,1,128]{2,0,1:T(8,128)(2,1)S(1)}, bf16[1024,1,128]{2,0,1:T(8,128)(2,1)}, u32[]{:S(2)}) copy-start(bf16[1024,1,128]{2,0,1:T(8,128)(2,1)} %get-tuple-element.59) | copy-start | bytes 786436
  153.0 9.5 %copy-start.42 = (bf16[1024,1,128]{2,0,1:T(8,128)(2,1)S(1)}, bf16[1024,1,128]{2,0,1:T(8,128)(2,1)}, u32[]{:S(2)}) copy-start(bf16[1024,1,128]{2,0,1:T(8,128)(2,1)} %get-tuple-element.60) | copy-start | bytes 786436
  153.0 9.5 %copy-start.43 = (bf16[1024,1,128]{2,0,1:T(8,128)(2,1)S(1)}, bf16[1024,1,128]{2,0,1:T(8,128)(2,1)}, u32[]{:S(2)}) copy-start(bf16[1024,1,128]{2,0,1:T(8,128)(2,1)} %get-tuple-element.57) | copy-start | bytes 786436
  157.2 39.3 %all-to-all-start.4 = ((bf16[2,1024,768]{2,1,0:T(8,128)(2,1)}), bf16[2,1024,768]{2,1,0:T(8,128)(2,1)}, u32[]{:S(2)}, u32[]{:S(2)}) async-start(bf16[2,1024,768]{2,1,0:T(8,128)(2,1)} %pad_maximum_fusion.1), calls=%async_computation.4 | async-start | bytes 6291456 | tf_op jit(solution)/shard_map/all_to_all | solution.py:174
  168.3 30.1 %copy-start.2 = (bf16[2,1024,8]{2,1,0:T(8,128)(2,1)S(1)}, bf16[2,1024,8]{2,1,0:T(8,128)(2,1)}, u32[]{:S(2)}) copy-start(bf16[2,1024,8]{2,1,0:T(8,128)(2,1)} %copy-done) | copy-start | bytes 98308
  168.3 30.1 %copy-start.4 = (bf16[2,1024,128]{2,1,0:T(8,128)(2,1)S(1)}, bf16[2,1024,128]{2,1,0:T(8,128)(2,1)}, u32[]{:S(2)}) copy-start(bf16[2,1024,128]{2,1,0:T(8,128)(2,1)} %dynamic-slice_bitcast_fusion.1.prompt_ref) | copy-start | bytes 1572868
  220.3 28.7 %all-to-all-start.5 = ((bf16[2,1024,256]{2,1,0:T(8,128)(2,1)}), bf16[2,1024,256]{2,1,0:T(8,128)(2,1)}, u32[]{:S(2)}, u32[]{:S(2)}) async-start(bf16[2,1024,256]{2,1,0:T(8,128)(2,1)} %bitcast.39), calls=%async_computation.5 | async-start | bytes 2097152 | tf_op jit(solution)/shard_map/all_to_all | solution.py:174
  224.9 21.1 %copy-start.29 = (bf16[2048,1,128]{2,0,1:T(8,128)(2,1)S(1)}, bf16[2048,1,128]{2,0,1:T(8,128)(2,1)}, u32[]{:S(2)}) copy-start(bf16[2048,1,128]{2,0,1:T(8,128)(2,1)} %slice_bitcast_fusion.3) | copy-start | bytes 1572868
  224.9 21.1 %copy-start.30 = (bf16[2048,1,128]{2,0,1:T(8,128)(2,1)S(1)}, bf16[2048,1,128]{2,0,1:T(8,128)(2,1)}, u32[]{:S(2)}) copy-start(bf16[2048,1,128]{2,0,1:T(8,128)(2,1)} %slice_bitcast_fusion.2) | copy-start | bytes 1572868
  224.9 21.1 %copy-start.31 = (bf16[2048,1,128]{2,0,1:T(8,128)(2,1)S(1)}, bf16[2048,1,128]{2,0,1:T(8,128)(2,1)}, u32[]{:S(2)}) copy-start(bf16[2048,1,128]{2,0,1:T(8,128)(2,1)} %slice_bitcast_fusion.1) | copy-start | bytes 1572868
  224.9 21.1 %copy-start.32 = (bf16[2048,1,128]{2,0,1:T(8,128)(2,1)S(1)}, bf16[2048,1,128]{2,0,1:T(8,128)(2,1)}, u32[]{:S(2)}) copy-start(bf16[2048,1,128]{2,0,1:T(8,128)(2,1)} %slice_bitcast_fusion) | copy-start | bytes 1572868
  249.0 55.8 %all-to-all-start.6 = ((bf16[2,1024,256]{2,1,0:T(8,128)(2,1)}), bf16[2,1024,256]{2,1,0:T(8,128)(2,1)}, u32[]{:S(2)}, u32[]{:S(2)}) async-start(bf16[2,1024,256]{2,1,0:T(8,128)(2,1)} %bitcast.43), calls=%async_computation.6 | async-start | bytes 2097152 | tf_op jit(solution)/shard_map/all_to_all | solution.py:174
  267.5 6.4 %copy-start.13 = (bf16[1,3072,4,128]{3,1,2,0:T(8,128)(2,1)S(1)}, bf16[1,3072,4,128]{3,1,2,0:T(8,128)(2,1)}, u32[]{:S(2)}) copy-start(bf16[1,3072,4,128]{3,1,2,0:T(8,128)(2,1)} %pad_bitcast_fusion.1) | copy-start | bytes 9437188
  (23 other events, 46.8 us)
Sparse Core Ops, SparseCore 0:
  11.1 44.1 all-gather.2
  57.5 40.0 all-gather.4
